TPU v7x, 32 devices: a whole 2x2x4 slice. The times are simulated.
32 devices in a mesh: group: 2 (over x), space: 16 (over z, y, core).
Axes of the slice: x: 2, y: 2, z: 4, core: 2. Of those that a mesh axis runs over, the one named last changes fastest.
Arguments:
- snapshots: bfloat16 [32, 3, 256, 128], P('group', None, 'space'), parts along dimension 0, may hold values from -8 to 8
- basis: bfloat16 [128, 3, 128, 256], P('group', None, 'space'), parts along dimension 0, may hold values from -6 to 6
- mode_weights: float32 [128], P('group'), parts along dimension 0, may hold values from 0.5 to 4
- land_mask: int32 [256, 128], P('space'), may hold values 0 or 1
- scale_index: int32 [128], replicated, may hold values from 0 to 15
- scale_values: float32 [16], replicated, may hold values from 0.06 to 0.24
Outputs:
- new_basis: bfloat16 [128, 3, 128, 256], P('group', None, 'space'), parts along dimension 0
- coefficients: float32 [32, 64], P('group'), parts along dimension 0
There are 2 independent parts, one for each index of `group`. A program takes and returns all parts, laid end to end along the dimension named above; an argument that names none is the same for every part. Nothing has to cross between parts.
Inputs may be any that keep to these rules, and one draw needn't show every extreme that they name: `land_mask`: 1 marks ocean, 0 land. Row y uses scale_values[scale_index[y]].
All inputs are finite; a program needn't handle non-finite values. No bound on the sum of `land_mask` on one device may be relied on, other than what follows from the above.
Results may differ from a plain program's by a relative error of at most 0.0057.
Values may be sent and summed in bfloat16 or wider, within the bound.
A program may use at most 128 MiB of HBM per device.

v0:
```python
import math
import jax
import jax.numpy as jnp
from jax import lax
from jax.sharding import PartitionSpec as P

PASS_COEFS = (1.0, 0.95, 0.85, 0.7, 0.5, 0.3)


def with_halo(cells, sides, width):
    for axis, dim in sides:
        count = lax.axis_size(axis)
        head = lax.slice_in_dim(cells, 0, width, axis=dim)
        tail = lax.slice_in_dim(cells, cells.shape[dim] - width, cells.shape[dim], axis=dim)
        cells = jnp.concatenate(
            [
                lax.ppermute(tail, axis, [(i, (i + 1) % count) for i in range(count)]),
                cells,
                lax.ppermute(head, axis, [((i + 1) % count, i) for i in range(count)]),
            ],
            axis=dim,
        )
    return cells


def latitude_scale(scale_index, scale_values):
    levels = jnp.arange(scale_values.shape[0], dtype=jnp.int32)
    matches = (scale_index[None, :] == levels[:, None]).astype(jnp.float32)
    return jnp.sum(matches * scale_values[:, None], axis=0)


def masked_step(fields_now, ocean, factor):
    centre = fields_now[:, :, 1:-1]
    m_centre = ocean[1:-1]
    east_flux = ocean[2:] * (fields_now[:, :, 2:] - centre)
    west_flux = ocean[:-2] * (fields_now[:, :, :-2] - centre)
    padded = jnp.pad(centre, ((0, 0), (0, 0), (0, 0), (1, 1)))
    m_pad = jnp.pad(m_centre, ((0, 0), (1, 1)))
    north_flux = m_pad[:, 2:] * (padded[..., 2:] - centre)
    south_flux = m_pad[:, :-2] * (padded[..., :-2] - centre)
    return centre + factor * (m_centre * (east_flux + west_flux + north_flux + south_flux))


def dot_rows(left, right):
    return lax.dot_general(
        left, right, (((1,), (1,)), ((), ())), preferred_element_type=jnp.float32
    )


def eof_update(data_rows, basis_rows, mode_weights, total_cells):
    high = lax.Precision.HIGHEST
    root_total = math.sqrt(total_cells)
    cross_sum = lax.psum(dot_rows(data_rows, basis_rows), "space")
    coefficients = cross_sum / root_total
    coeff_b = coefficients.astype(jnp.bfloat16)
    update = mode_weights[:, None] * basis_rows.astype(jnp.float32) + lax.dot_general(
        coeff_b, data_rows, (((0,), (0,)), ((), ())), preferred_element_type=jnp.float32
    )
    gram_matrix = lax.psum(jnp.dot(update, update.T, precision=high), "space") / total_cells
    chol_factor = jnp.linalg.cholesky(gram_matrix)
    solved = jax.scipy.linalg.solve_triangular(chol_factor, update, lower=True)
    return (solved.astype(jnp.bfloat16), coefficients)


def local(snapshots, basis, mode_weights, land_mask, scale_index, scale_values):
    lat_scale = latitude_scale(scale_index, scale_values)
    halo_width = 1
    ocean_wide = with_halo(land_mask, (("space", 0),), halo_width).astype(jnp.float32)
    fields_now = snapshots.astype(jnp.float32)
    for group_start in range(0, len(PASS_COEFS), halo_width):
        extended = with_halo(fields_now, (("space", 2),), 1)
        factor = PASS_COEFS[group_start] * lat_scale
        extended = masked_step(extended, ocean_wide, factor)
        fields_now = extended
    ocean = land_mask.astype(jnp.float32)
    filtered = (ocean * fields_now).astype(jnp.bfloat16)
    modes = basis.shape[0]
    snaps = filtered.shape[0]
    slab_data = lax.all_to_all(filtered, "space", split_axis=3, concat_axis=2, tiled=True)
    data_rows = jnp.swapaxes(slab_data, 2, 3).reshape(snaps, -1)
    basis_rows = basis.reshape(modes, -1)
    total_cells = float(data_rows.shape[1] * lax.axis_size("space"))
    solved, coefficients = eof_update(data_rows, basis_rows, mode_weights, total_cells)
    new_basis = solved.reshape(basis.shape)
    return (new_basis, coefficients)


def solution(mesh):
    placed = (
        P("group", None, "space", None),
        P("group", None, "space", None),
        P("group"),
        P("space", None),
        P(),
        P(),
    )
    return jax.shard_map(
        local,
        mesh=mesh,
        in_specs=placed,
        out_specs=(P("group", None, "space", None), P("group", None)),
        check_vma=False,
    )
```

profile of v0, /device:TPU:0, one launch (start us, length us, event | category | flops | bytes accessed | tf_op | source)
XLA Modules:
  0.0 175.6 jit_solution(13503581497344326809)
XLA Ops:
  0.6 0.7 fusion.94
  1.8 5.0 %collective-permute-start.1 = (s32[1,128]{1,0:T(1,128)S(1)}, s32[1,128]{1,0:T(1,128)S(1)}, u32[]{:S(2)}, u32[]{:S(2)}) collective-permute-start(s32[1,128]{1,0:T(1,128)S(1)} %get-tuple-element.20), channel_id=1, source_target_pairs={{1,0},{2,1},{3,2},{4,3},{5,4},{6,5},{7,6},{8,7},{9,8},{10,9},{11,1... | collective-permute-start | bytes 1544 | tf_op jit(solution)/shard_map/ppermute | solution.py:19
  6.8 1.0 copy_convert_fusion
  7.8 0.7 collective-permute-start.2
  8.5 0.7 add_convert_fusion
  9.2 0.8 pad_slice_fusion.13
  10.0 4.4 %collective-permute-done.3 = f32[16,3,1,128]{3,0,2,1:T(8,128)S(1)} collective-permute-done((f32[16,3,1,128]{3,0,2,1:T(8,128)S(1)}, f32[16,3,1,128]{3,0,2,1:T(8,128)S(1)}, u32[]{:S(2)}, u32[]{:S(2)}) %collective-permute-start.3) | collective-permute-done | bytes 24608 | tf_op jit(solution)/shard_map/ppermute | solution.py:17
  14.4 1.2 convert_add_fusion
  16.3 1.0 collective-permute-done.4
  17.3 4.6 %collective-permute-done.5 = f32[16,3,1,128]{3,0,2,1:T(8,128)S(1)} collective-permute-done((f32[16,3,1,128]{3,0,2,1:T(8,128)S(1)}, f32[16,3,1,128]{3,0,2,1:T(8,128)S(1)}, u32[]{:S(2)}, u32[]{:S(2)}) %collective-permute-start.5) | collective-permute-done | bytes 24608 | tf_op jit(solution)/shard_map/ppermute | solution.py:17
  22.7 1.0 collective-permute-done.6
  23.7 4.5 %collective-permute-done.7 = f32[16,3,1,128]{3,0,2,1:T(8,128)S(1)} collective-permute-done((f32[16,3,1,128]{3,0,2,1:T(8,128)S(1)}, f32[16,3,1,128]{3,0,2,1:T(8,128)S(1)}, u32[]{:S(2)}, u32[]{:S(2)}) %collective-permute-start.7) | collective-permute-done | bytes 24608 | tf_op jit(solution)/shard_map/ppermute | solution.py:17
  29.1 1.0 collective-permute-done.8
  30.1 4.5 %collective-permute-done.9 = f32[16,3,1,128]{3,0,2,1:T(8,128)S(1)} collective-permute-done((f32[16,3,1,128]{3,0,2,1:T(8,128)S(1)}, f32[16,3,1,128]{3,0,2,1:T(8,128)S(1)}, u32[]{:S(2)}, u32[]{:S(2)}) %collective-permute-start.9) | collective-permute-done | bytes 24608 | tf_op jit(solution)/shard_map/ppermute | solution.py:17
  35.5 1.0 collective-permute-done.10
  36.6 4.5 %collective-permute-done.11 = f32[16,3,1,128]{3,0,2,1:T(8,128)S(1)} collective-permute-done((f32[16,3,1,128]{3,0,2,1:T(8,128)S(1)}, f32[16,3,1,128]{3,0,2,1:T(8,128)S(1)}, u32[]{:S(2)}, u32[]{:S(2)}) %collective-permute-start.11) | collective-permute-done | bytes 24608 | tf_op jit(solution)/shard_map/ppermute | solution.py:17
  42.0 1.0 collective-permute-done.12
  43.0 4.5 %collective-permute-done.13 = f32[16,3,1,128]{3,0,2,1:T(8,128)S(1)} collective-permute-done((f32[16,3,1,128]{3,0,2,1:T(8,128)S(1)}, f32[16,3,1,128]{3,0,2,1:T(8,128)S(1)}, u32[]{:S(2)}, u32[]{:S(2)}) %collective-permute-start.13) | collective-permute-done | bytes 24608 | tf_op jit(solution)/shard_map/ppermute | solution.py:17
  47.8 1.1 copy.41
  48.9 2.3 %reshape.52 = bf16[16,2,3072]{2,1,0:T(2,128)(2,1)} reshape(bf16[128,3,16,16]{3,2,1,0:T(8,128)(2,1)S(1)} %bitcast.42) | data formatting | bytes 393216
  51.2 3.5 %all-to-all-start = ((bf16[16,2,3072]{2,1,0:T(2,128)(2,1)}), bf16[16,2,3072]{2,1,0:T(2,128)(2,1)S(1)}, u32[]{:S(2)}, u32[]{:S(2)}) async-start(bf16[16,2,3072]{2,1,0:T(2,128)(2,1)} %reshape.52), calls=%async_computation | async-start | bytes 393216 | tf_op jit(solution)/shard_map/all_to_all | solution.py:79
  54.9 8.8 %all-to-all-done = bf16[16,2,3072]{2,1,0:T(2,128)(2,1)S(1)} async-done(((bf16[16,2,3072]{2,1,0:T(2,128)(2,1)}), bf16[16,2,3072]{2,1,0:T(2,128)(2,1)S(1)}, u32[]{:S(2)}, u32[]{:S(2)}) %all-to-all-start) | async-done | bytes 196640 | tf_op jit(solution)/shard_map/all_to_all | solution.py:79
  63.7 1.2 reshape.53
  64.9 2.2 %copy.43 = bf16[16,3,16,16,8]{3,2,0,4,1:T(8,128)(2,1)} copy(bf16[16,3,16,16,8]{3,0,1,4,2:T(8,128)(2,1)S(1)} %bitcast.43) | data formatting | bytes 393216 | tf_op jit(solution)/shard_map/all_to_all | solution.py:79
  67.1 2.7 %all_to_all.16 = bf16[16,3,256,8]{2,0,3,1:T(8,128)(2,1)S(1)} reshape(bf16[16,3,16,16,8]{3,2,0,4,1:T(8,128)(2,1)} %copy.43) | data formatting | bytes 393216 | tf_op jit(solution)/shard_map/all_to_all | solution.py:79
  70.1 31.0 %psum.14 = f32[16,64]{1,0:T(8,128)S(1)} all-reduce(f32[16,64]{1,0:T(8,128)S(1)} %convolution_bitcast_fusion), channel_id=1, replica_groups=mesh['group'=2,'space'=16] {'space'}, use_global_device_ids=true, to_apply=%region_1.2 | all-reduce | flops 1024 | bytes 8192 | tf_op jit(solution)/shard_map/psum | solution.py:53
  101.7 1.4 fusion.95
  103.1 57.8 %psum.15 = f32[64,64]{0,1:T(8,128)S(1)} all-reduce(f32[64,64]{0,1:T(8,128)S(1)} %fusion.95), channel_id=1, replica_groups=mesh['group'=2,'space'=16] {'space'}, use_global_device_ids=true, to_apply=%region_2.3 | all-reduce | flops 4096 | bytes 32768 | tf_op jit(solution)/shard_map/psum | solution.py:59
  161.0 5.8 %cholesky.16 = f32[64,64]{1,0:T(8,128)S(1)} custom-call(f32[64,64]{1,0:T(8,128)S(1)} %fusion.84), custom_call_target="Cholesky" | custom-call | tf_op jit(solution)/shard_map/jit(cholesky)/cholesky | solution.py:60
  168.2 4.9 %custom-call.7 = f32[1,64,64]{1,2,0:T(8,128)S(1)} custom-call(f32[1,64,64]{2,1,0:T(8,128)S(1)} %fusion.82), custom_call_target="InvertDiagBlocksLowerTriangular" | custom-call | tf_op jit(solution)/shard_map/jit(_solve_triangular)/triangular_solve | solution.py:61
  173.1 1.5 convolution_convert_fusion
  174.6 1.0 copy.53
  (50 shorter events, 7.2 us)
Async XLA Ops:
  1.3 7.2 %collective-permute-start = (s32[1,128]{1,0:T(1,128)S(1)}, s32[1,128]{1,0:T(1,128)S(1)}, u32[]{:S(2)}, u32[]{:S(2)}) collective-permute-start(s32[1,128]{1,0:T(1,128)S(1)} %get-tuple-element.19), channel_id=1, source_target_pairs={{0,1},{1,2},{2,3},{3,4},{4,5},{5,6},{6,7},{7,8},{8,9},{9,10},{10,1... | collective-permute-start | bytes 1544 | tf_op jit(solution)/shard_map/ppermute | solution.py:17
  1.8 6.7 %collective-permute-start.1 = (s32[1,128]{1,0:T(1,128)S(1)}, s32[1,128]{1,0:T(1,128)S(1)}, u32[]{:S(2)}, u32[]{:S(2)}) collective-permute-start(s32[1,128]{1,0:T(1,128)S(1)} %get-tuple-element.20), channel_id=1, source_target_pairs={{1,0},{2,1},{3,2},{4,3},{5,4},{6,5},{7,6},{8,7},{9,8},{10,9},{11,1... | collective-permute-start | bytes 1544 | tf_op jit(solution)/shard_map/ppermute | solution.py:19
  7.8 2.2 %collective-permute-start.2 = (f32[16,3,1,128]{3,0,2,1:T(8,128)S(1)}, f32[16,3,1,128]{3,0,2,1:T(8,128)S(1)}, u32[]{:S(2)}, u32[]{:S(2)}) collective-permute-start(f32[16,3,1,128]{3,0,2,1:T(8,128)S(1)} %get-tuple-element.12), channel_id=1, source_target_pairs={{1,0},{2,1},{3,2},{4,3},{5,4},{6,5},{7,6},{8,7},{9,8},{10,9},{11,1... | collective-permute-start | bytes 73736 | tf_op jit(solution)/shard_map/ppermute | solution.py:19
  8.5 5.9 %collective-permute-start.3 = (f32[16,3,1,128]{3,0,2,1:T(8,128)S(1)}, f32[16,3,1,128]{3,0,2,1:T(8,128)S(1)}, u32[]{:S(2)}, u32[]{:S(2)}) collective-permute-start(f32[16,3,1,128]{3,0,2,1:T(8,128)S(1)} %get-tuple-element.13), channel_id=1, source_target_pairs={{0,1},{1,2},{2,3},{3,4},{4,5},{5,6},{6,7},{7,8},{8,9},{9,10},{10,1... | collective-permute-start | bytes 73736 | tf_op jit(solution)/shard_map/ppermute | solution.py:17
  15.7 1.6 collective-permute-start.4
  15.8 6.1 %collective-permute-start.5 = (f32[16,3,1,128]{3,0,2,1:T(8,128)S(1)}, f32[16,3,1,128]{3,0,2,1:T(8,128)S(1)}, u32[]{:S(2)}, u32[]{:S(2)}) collective-permute-start(f32[16,3,1,128]{3,0,2,1:T(8,128)S(1)} %get-tuple-element.11), channel_id=1, source_target_pairs={{0,1},{1,2},{2,3},{3,4},{4,5},{5,6},{6,7},{7,8},{8,9},{9,10},{10,1... | collective-permute-start | bytes 73736 | tf_op jit(solution)/shard_map/ppermute | solution.py:17
  22.1 19.9 %copy-start.2 = (s32[16,128]{1,0:T(8,128)S(1)}, s32[16,128]{1,0:T(8,128)}, u32[]{:S(2)}) copy-start(s32[16,128]{1,0:T(8,128)} %param.9) | copy-start | bytes 24580
  22.1 1.6 collective-permute-start.6
  22.2 6.1 %collective-permute-start.7 = (f32[16,3,1,128]{3,0,2,1:T(8,128)S(1)}, f32[16,3,1,128]{3,0,2,1:T(8,128)S(1)}, u32[]{:S(2)}, u32[]{:S(2)}) collective-permute-start(f32[16,3,1,128]{3,0,2,1:T(8,128)S(1)} %get-tuple-element.9), channel_id=1, source_target_pairs={{0,1},{1,2},{2,3},{3,4},{4,5},{5,6},{6,7},{7,8},{8,9},{9,10},{10,1... | collective-permute-start | bytes 73736 | tf_op jit(solution)/shard_map/ppermute | solution.py:17
  28.6 1.6 collective-permute-start.8
  28.6 6.1 %collective-permute-start.9 = (f32[16,3,1,128]{3,0,2,1:T(8,128)S(1)}, f32[16,3,1,128]{3,0,2,1:T(8,128)S(1)}, u32[]{:S(2)}, u32[]{:S(2)}) collective-permute-start(f32[16,3,1,128]{3,0,2,1:T(8,128)S(1)} %get-tuple-element.7), channel_id=1, source_target_pairs={{0,1},{1,2},{2,3},{3,4},{4,5},{5,6},{6,7},{7,8},{8,9},{9,10},{10,1... | collective-permute-start | bytes 73736 | tf_op jit(solution)/shard_map/ppermute | solution.py:17
  35.0 1.6 collective-permute-start.10
  35.1 6.1 %collective-permute-start.11 = (f32[16,3,1,128]{3,0,2,1:T(8,128)S(1)}, f32[16,3,1,128]{3,0,2,1:T(8,128)S(1)}, u32[]{:S(2)}, u32[]{:S(2)}) collective-permute-start(f32[16,3,1,128]{3,0,2,1:T(8,128)S(1)} %get-tuple-element.5), channel_id=1, source_target_pairs={{0,1},{1,2},{2,3},{3,4},{4,5},{5,6},{6,7},{7,8},{8,9},{9,10},{10,1... | collective-permute-start | bytes 73736 | tf_op jit(solution)/shard_map/ppermute | solution.py:17
  41.4 1.6 collective-permute-start.12
  41.5 6.0 %collective-permute-start.13 = (f32[16,3,1,128]{3,0,2,1:T(8,128)S(1)}, f32[16,3,1,128]{3,0,2,1:T(8,128)S(1)}, u32[]{:S(2)}, u32[]{:S(2)}) collective-permute-start(f32[16,3,1,128]{3,0,2,1:T(8,128)S(1)} %get-tuple-element.3), channel_id=1, source_target_pairs={{0,1},{1,2},{2,3},{3,4},{4,5},{5,6},{6,7},{7,8},{8,9},{9,10},{10,1... | collective-permute-start | bytes 73736 | tf_op jit(solution)/shard_map/ppermute | solution.py:17
  47.8 7.0 %copy-start = (bf16[64,3,8,256]{3,2,1,0:T(8,128)(2,1)S(1)}, bf16[64,3,8,256]{3,2,1,0:T(8,128)(2,1)}, u32[]{:S(2)}) copy-start(bf16[64,3,8,256]{3,2,1,0:T(8,128)(2,1)} %param.7) | copy-start | bytes 2359300
  51.2 12.5 %all-to-all-start = ((bf16[16,2,3072]{2,1,0:T(2,128)(2,1)}), bf16[16,2,3072]{2,1,0:T(2,128)(2,1)S(1)}, u32[]{:S(2)}, u32[]{:S(2)}) async-start(bf16[16,2,3072]{2,1,0:T(2,128)(2,1)} %reshape.52), calls=%async_computation | async-start | bytes 393216 | tf_op jit(solution)/shard_map/all_to_all | solution.py:79
  67.1 2.7 %copy-start.1 = (bf16[64,3,8,256]{3,2,1,0:T(8,128)(2,1)S(1)}, bf16[64,3,8,256]{3,2,1,0:T(8,128)(2,1)}, u32[]{:S(2)}) copy-start(bf16[64,3,8,256]{3,2,1,0:T(8,128)(2,1)} %param.7) | copy-start | bytes 2359300
  67.1 34.0 %copy-start.4 = (f32[64]{0:T(128)S(1)}, f32[64]{0:T(128)}, u32[]{:S(2)}) copy-start(f32[64]{0:T(128)} %param.8) | copy-start | bytes 772
  101.1 0.6 copy-start.3
where the time goes:
time: 176 us
  blocking collectives  88.8 us (50%)
  waiting for transfers between devices  41 us (23%)
  other arithmetic  17.2 us (10%)
  starting transfers between devices  12.5 us (7%)
  local copies, waits for them, and re-layouts  11.7 us (7%)
  matrix products  3.56 us (2%)
    psum x1, blocking collectives, eof_update(): lax.psum(jnp.dot(update, update.T, precision=high), 'space') / total_cells  57.8 us
    psum x1, blocking collectives, eof_update(): cross_sum = lax.psum(dot_rows(data_rows, basis_rows), 'space')  31 us
    ppermute x7, waiting for transfers between devices, with_halo(): lax.ppermute(tail, axis, [(i, (i + 1) % count) for i in range(count)])  27.1 us
    all_to_all x1, waiting for transfers between devices, local(): lax.all_to_all(filtered, 'space', split_axis=3, concat_axis=2, tiled=True)  8.79 us
    another operation x3, other arithmetic, eof_update(): chol_factor = jnp.linalg.cholesky(gram_matrix)  6.52 us
    ppermute x7, starting transfers between devices, with_halo(): lax.ppermute(head, axis, [((i + 1) % count, i) for i in range(count)])  6.01 us
    another operation x2, other arithmetic, eof_update(): solved = jax.scipy.linalg.solve_triangular(chol_factor, update, lower=True)  5.55 us
    ppermute x7, waiting for transfers between devices, with_halo(): lax.ppermute(head, axis, [((i + 1) % count, i) for i in range(count)])  5.11 us
  transfers between devices with their start and end apart: 15, of which 12 were waited for; matrix products, arithmetic and copies ran while one was open for 1% of the time, Pallas kernels for 0%

commit v1 on v0

--- a/solution.py
+++ b/solution.py
@@ -56,7 +56,10 @@
     update = mode_weights[:, None] * basis_rows.astype(jnp.float32) + lax.dot_general(
         coeff_b, data_rows, (((0,), (0,)), ((), ())), preferred_element_type=jnp.float32
     )
-    gram_matrix = lax.psum(jnp.dot(update, update.T, precision=high), "space") / total_cells
+    gram_matrix = (
+        jnp.sum(lax.all_gather(jnp.dot(update, update.T, precision=high), "space"), axis=0)
+        / total_cells
+    )
     chol_factor = jnp.linalg.cholesky(gram_matrix)
     solved = jax.scipy.linalg.solve_triangular(chol_factor, update, lower=True)
     return (solved.astype(jnp.bfloat16), coefficients)

time: 176 us -> 137 us (0.78)
  blocking collectives: 88.8 us -> 50 us
    psum x1 -> x0, blocking collectives: 57.8 us -> none  [eof_update(): lax.psum(jnp.dot(update, update.T, precision=high), 'space') / total_cells]
    all_gather x0 -> x1, blocking collectives: none -> 19 us  [eof_update(): lax.all_gather(jnp.dot(update, update.T, precision=high), 'space')]
    unnamed x15 -> x13, local copies, waits for them, and re-layouts: 4.89 us -> 6.02 us
  transfers between devices with their start and end apart: 15 -> 15, of which waited for: 12 -> 12; matrix products, arithmetic and copies ran while one was open for 1% -> 3% of each run, Pallas kernels for 0% -> 0%
where the time goes in v1:
time: 137 us
  blocking collectives  50 us (36%)
  waiting for transfers between devices  39.9 us (29%)
  other arithmetic  17.2 us (13%)
  local copies, waits for them, and re-layouts  12.9 us (9%)
  starting transfers between devices  12.5 us (9%)
  matrix products  3.56 us (3%)
    psum x1, blocking collectives, eof_update(): cross_sum = lax.psum(dot_rows(data_rows, basis_rows), 'space')  31 us
    ppermute x7, waiting for transfers between devices, with_halo(): lax.ppermute(tail, axis, [(i, (i + 1) % count) for i in range(count)])  27.1 us
    all_gather x1, blocking collectives, eof_update(): lax.all_gather(jnp.dot(update, update.T, precision=high), 'space')  19 us
    all_to_all x1, waiting for transfers between devices, local(): lax.all_to_all(filtered, 'space', split_axis=3, concat_axis=2, tiled=True)  7.67 us
    another operation x3, other arithmetic, eof_update(): chol_factor = jnp.linalg.cholesky(gram_matrix)  6.52 us
    unnamed x13, local copies, waits for them, and re-layouts  6.02 us
    ppermute x7, starting transfers between devices, with_halo(): lax.ppermute(head, axis, [((i + 1) % count, i) for i in range(count)])  6.01 us
    another operation x2, other arithmetic, eof_update(): solved = jax.scipy.linalg.solve_triangular(chol_factor, update, lower=True)  5.55 us
  transfers between devices with their start and end apart: 15, of which 12 were waited for; matrix products, arithmetic and copies ran while one was open for 3% of the time, Pallas kernels for 0%

profile of v1, /device:TPU:0, one launch (start us, length us, event | category | flops | bytes accessed | tf_op | source)
XLA Modules:
  0.0 136.9 jit_solution(10889309395529327780)
XLA Ops:
  0.6 0.7 fusion.94
  1.8 5.0 %collective-permute-start.1 = (s32[1,128]{1,0:T(1,128)S(1)}, s32[1,128]{1,0:T(1,128)S(1)}, u32[]{:S(2)}, u32[]{:S(2)}) collective-permute-start(s32[1,128]{1,0:T(1,128)S(1)} %get-tuple-element.20), channel_id=1, source_target_pairs={{1,0},{2,1},{3,2},{4,3},{5,4},{6,5},{7,6},{8,7},{9,8},{10,9},{11,1... | collective-permute-start | bytes 1544 | tf_op jit(solution)/shard_map/ppermute | solution.py:19
  6.8 1.0 copy_convert_fusion
  7.8 0.7 collective-permute-start.2
  9.2 0.8 pad_slice_fusion.13
  10.0 4.4 %collective-permute-done.3 = f32[16,3,1,128]{3,0,2,1:T(8,128)S(1)} collective-permute-done((f32[16,3,1,128]{3,0,2,1:T(8,128)S(1)}, f32[16,3,1,128]{3,0,2,1:T(8,128)S(1)}, u32[]{:S(2)}, u32[]{:S(2)}) %collective-permute-start.3) | collective-permute-done | bytes 24608 | tf_op jit(solution)/shard_map/ppermute | solution.py:17
  14.4 1.2 convert_add_fusion
  16.3 1.0 collective-permute-done.4
  17.3 4.6 %collective-permute-done.5 = f32[16,3,1,128]{3,0,2,1:T(8,128)S(1)} collective-permute-done((f32[16,3,1,128]{3,0,2,1:T(8,128)S(1)}, f32[16,3,1,128]{3,0,2,1:T(8,128)S(1)}, u32[]{:S(2)}, u32[]{:S(2)}) %collective-permute-start.5) | collective-permute-done | bytes 24608 | tf_op jit(solution)/shard_map/ppermute | solution.py:17
  22.7 1.0 collective-permute-done.6
  23.7 4.5 %collective-permute-done.7 = f32[16,3,1,128]{3,0,2,1:T(8,128)S(1)} collective-permute-done((f32[16,3,1,128]{3,0,2,1:T(8,128)S(1)}, f32[16,3,1,128]{3,0,2,1:T(8,128)S(1)}, u32[]{:S(2)}, u32[]{:S(2)}) %collective-permute-start.7) | collective-permute-done | bytes 24608 | tf_op jit(solution)/shard_map/ppermute | solution.py:17
  29.1 1.0 collective-permute-done.8
  30.1 4.5 %collective-permute-done.9 = f32[16,3,1,128]{3,0,2,1:T(8,128)S(1)} collective-permute-done((f32[16,3,1,128]{3,0,2,1:T(8,128)S(1)}, f32[16,3,1,128]{3,0,2,1:T(8,128)S(1)}, u32[]{:S(2)}, u32[]{:S(2)}) %collective-permute-start.9) | collective-permute-done | bytes 24608 | tf_op jit(solution)/shard_map/ppermute | solution.py:17
  35.5 1.0 collective-permute-done.10
  36.6 4.5 %collective-permute-done.11 = f32[16,3,1,128]{3,0,2,1:T(8,128)S(1)} collective-permute-done((f32[16,3,1,128]{3,0,2,1:T(8,128)S(1)}, f32[16,3,1,128]{3,0,2,1:T(8,128)S(1)}, u32[]{:S(2)}, u32[]{:S(2)}) %collective-permute-start.11) | collective-permute-done | bytes 24608 | tf_op jit(solution)/shard_map/ppermute | solution.py:17
  42.0 1.0 collective-permute-done.12
  43.0 4.5 %collective-permute-done.13 = f32[16,3,1,128]{3,0,2,1:T(8,128)S(1)} collective-permute-done((f32[16,3,1,128]{3,0,2,1:T(8,128)S(1)}, f32[16,3,1,128]{3,0,2,1:T(8,128)S(1)}, u32[]{:S(2)}, u32[]{:S(2)}) %collective-permute-start.13) | collective-permute-done | bytes 24608 | tf_op jit(solution)/shard_map/ppermute | solution.py:17
  47.8 1.1 copy.39
  48.9 2.3 %reshape.53 = bf16[16,2,3072]{2,1,0:T(2,128)(2,1)} reshape(bf16[128,3,16,16]{3,2,1,0:T(8,128)(2,1)S(1)} %bitcast.43) | data formatting | bytes 393216
  51.2 3.5 %all-to-all-start = ((bf16[16,2,3072]{2,1,0:T(2,128)(2,1)}), bf16[16,2,3072]{2,1,0:T(2,128)(2,1)S(1)}, u32[]{:S(2)}, u32[]{:S(2)}) async-start(bf16[16,2,3072]{2,1,0:T(2,128)(2,1)} %reshape.53), calls=%async_computation | async-start | bytes 393216 | tf_op jit(solution)/shard_map/all_to_all | solution.py:82
  54.8 1.3 copy.48
  56.1 7.7 %all-to-all-done = bf16[16,2,3072]{2,1,0:T(2,128)(2,1)S(1)} async-done(((bf16[16,2,3072]{2,1,0:T(2,128)(2,1)}), bf16[16,2,3072]{2,1,0:T(2,128)(2,1)S(1)}, u32[]{:S(2)}, u32[]{:S(2)}) %all-to-all-start) | async-done | bytes 196640 | tf_op jit(solution)/shard_map/all_to_all | solution.py:82
  63.7 1.2 reshape.54
  64.9 2.2 %copy.41 = bf16[16,3,16,16,8]{3,2,0,4,1:T(8,128)(2,1)} copy(bf16[16,3,16,16,8]{3,0,1,4,2:T(8,128)(2,1)S(1)} %bitcast.44) | data formatting | bytes 393216 | tf_op jit(solution)/shard_map/all_to_all | solution.py:82
  67.1 2.7 %all_to_all.16 = bf16[16,3,256,8]{2,0,3,1:T(8,128)(2,1)S(1)} reshape(bf16[16,3,16,16,8]{3,2,0,4,1:T(8,128)(2,1)} %copy.41) | data formatting | bytes 393216 | tf_op jit(solution)/shard_map/all_to_all | solution.py:82
  70.1 31.0 %psum.7 = f32[16,64]{1,0:T(8,128)S(1)} all-reduce(f32[16,64]{1,0:T(8,128)S(1)} %convolution_bitcast_fusion), channel_id=1, replica_groups=mesh['group'=2,'space'=16] {'space'}, use_global_device_ids=true, to_apply=%region_1.2 | all-reduce | flops 1024 | bytes 8192 | tf_op jit(solution)/shard_map/psum | solution.py:53
  101.7 1.4 %fusion.95 = f32[64,64]{1,0:T(8,128)S(1)} fusion(f32[64,6144]{1,0:T(8,128)S(1)} %convolution_add_fusion), kind=kOutput, calls=%fused_computation.146 | convolution fusion | flops 301989888 | bytes 1589248 | tf_op jit(solution)/shard_map/dot_general | solution.py:60
  103.0 19.0 %all-gather = f32[1024,64]{1,0:T(8,128)S(1)} all-gather(f32[64,64]{1,0:T(8,128)S(1)} %fusion.95), channel_id=2, replica_groups=mesh['group'=2,'space'=16] {'space'}, dimensions={0}, use_global_device_ids=true | all-gather | bytes 278528 | tf_op jit(solution)/shard_map/all_gather | solution.py:60
  122.3 5.8 %cholesky.16 = f32[64,64]{1,0:T(8,128)S(1)} custom-call(f32[64,64]{1,0:T(8,128)S(1)} %fusion.84), custom_call_target="Cholesky" | custom-call | tf_op jit(solution)/shard_map/jit(cholesky)/cholesky | solution.py:63
  129.5 4.9 %custom-call.7 = f32[1,64,64]{1,2,0:T(8,128)S(1)} custom-call(f32[1,64,64]{2,1,0:T(8,128)S(1)} %fusion.82), custom_call_target="InvertDiagBlocksLowerTriangular" | custom-call | tf_op jit(solution)/shard_map/jit(_solve_triangular)/triangular_solve | solution.py:64
  134.4 1.5 %convolution_convert_fusion = bf16[64,6144]{1,0:T(8,128)(2,1)S(1)} fusion(f32[64,6144]{1,0:T(8,128)S(1)} %convolution_add_fusion, f32[1,64,64]{1,2,0:T(8,128)S(1)} %custom-call.7), kind=kOutput, calls=%fused_computation.1 | convolution fusion | flops 302383104 | bytes 2375680 | tf_op jit(solution)/shard_map/jit(_solve_triangular)/triangular_solve | solution.py:64
  135.8 1.0 copy.50
  (50 shorter events, 7.9 us)
Async XLA Ops:
  1.3 7.2 %collective-permute-start = (s32[1,128]{1,0:T(1,128)S(1)}, s32[1,128]{1,0:T(1,128)S(1)}, u32[]{:S(2)}, u32[]{:S(2)}) collective-permute-start(s32[1,128]{1,0:T(1,128)S(1)} %get-tuple-element.19), channel_id=1, source_target_pairs={{0,1},{1,2},{2,3},{3,4},{4,5},{5,6},{6,7},{7,8},{8,9},{9,10},{10,1... | collective-permute-start | bytes 1544 | tf_op jit(solution)/shard_map/ppermute | solution.py:17
  1.8 6.7 %collective-permute-start.1 = (s32[1,128]{1,0:T(1,128)S(1)}, s32[1,128]{1,0:T(1,128)S(1)}, u32[]{:S(2)}, u32[]{:S(2)}) collective-permute-start(s32[1,128]{1,0:T(1,128)S(1)} %get-tuple-element.20), channel_id=1, source_target_pairs={{1,0},{2,1},{3,2},{4,3},{5,4},{6,5},{7,6},{8,7},{9,8},{10,9},{11,1... | collective-permute-start | bytes 1544 | tf_op jit(solution)/shard_map/ppermute | solution.py:19
  7.8 2.2 %collective-permute-start.2 = (f32[16,3,1,128]{3,0,2,1:T(8,128)S(1)}, f32[16,3,1,128]{3,0,2,1:T(8,128)S(1)}, u32[]{:S(2)}, u32[]{:S(2)}) collective-permute-start(f32[16,3,1,128]{3,0,2,1:T(8,128)S(1)} %get-tuple-element.12), channel_id=1, source_target_pairs={{1,0},{2,1},{3,2},{4,3},{5,4},{6,5},{7,6},{8,7},{9,8},{10,9},{11,1... | collective-permute-start | bytes 73736 | tf_op jit(solution)/shard_map/ppermute | solution.py:19
  8.5 5.9 %collective-permute-start.3 = (f32[16,3,1,128]{3,0,2,1:T(8,128)S(1)}, f32[16,3,1,128]{3,0,2,1:T(8,128)S(1)}, u32[]{:S(2)}, u32[]{:S(2)}) collective-permute-start(f32[16,3,1,128]{3,0,2,1:T(8,128)S(1)} %get-tuple-element.13), channel_id=1, source_target_pairs={{0,1},{1,2},{2,3},{3,4},{4,5},{5,6},{6,7},{7,8},{8,9},{9,10},{10,1... | collective-permute-start | bytes 73736 | tf_op jit(solution)/shard_map/ppermute | solution.py:17
  15.7 1.6 %collective-permute-start.4 = (f32[16,3,1,128]{3,0,2,1:T(8,128)S(1)}, f32[16,3,1,128]{3,0,2,1:T(8,128)S(1)}, u32[]{:S(2)}, u32[]{:S(2)}) collective-permute-start(f32[16,3,1,128]{3,0,2,1:T(8,128)S(1)} %get-tuple-element.10), channel_id=1, source_target_pairs={{1,0},{2,1},{3,2},{4,3},{5,4},{6,5},{7,6},{8,7},{9,8},{10,9},{11,1... | collective-permute-start | bytes 73736 | tf_op jit(solution)/shard_map/ppermute | solution.py:19
  15.8 6.1 %collective-permute-start.5 = (f32[16,3,1,128]{3,0,2,1:T(8,128)S(1)}, f32[16,3,1,128]{3,0,2,1:T(8,128)S(1)}, u32[]{:S(2)}, u32[]{:S(2)}) collective-permute-start(f32[16,3,1,128]{3,0,2,1:T(8,128)S(1)} %get-tuple-element.11), channel_id=1, source_target_pairs={{0,1},{1,2},{2,3},{3,4},{4,5},{5,6},{6,7},{7,8},{8,9},{9,10},{10,1... | collective-permute-start | bytes 73736 | tf_op jit(solution)/shard_map/ppermute | solution.py:17
  22.1 19.9 %copy-start.1 = (s32[16,128]{1,0:T(8,128)S(1)}, s32[16,128]{1,0:T(8,128)}, u32[]{:S(2)}) copy-start(s32[16,128]{1,0:T(8,128)} %param.9) | copy-start | bytes 24580
  22.1 1.6 %collective-permute-start.6 = (f32[16,3,1,128]{3,0,2,1:T(8,128)S(1)}, f32[16,3,1,128]{3,0,2,1:T(8,128)S(1)}, u32[]{:S(2)}, u32[]{:S(2)}) collective-permute-start(f32[16,3,1,128]{3,0,2,1:T(8,128)S(1)} %get-tuple-element.8), channel_id=1, source_target_pairs={{1,0},{2,1},{3,2},{4,3},{5,4},{6,5},{7,6},{8,7},{9,8},{10,9},{11,1... | collective-permute-start | bytes 73736 | tf_op jit(solution)/shard_map/ppermute | solution.py:19
  22.2 6.1 %collective-permute-start.7 = (f32[16,3,1,128]{3,0,2,1:T(8,128)S(1)}, f32[16,3,1,128]{3,0,2,1:T(8,128)S(1)}, u32[]{:S(2)}, u32[]{:S(2)}) collective-permute-start(f32[16,3,1,128]{3,0,2,1:T(8,128)S(1)} %get-tuple-element.9), channel_id=1, source_target_pairs={{0,1},{1,2},{2,3},{3,4},{4,5},{5,6},{6,7},{7,8},{8,9},{9,10},{10,1... | collective-permute-start | bytes 73736 | tf_op jit(solution)/shard_map/ppermute | solution.py:17
  28.6 1.6 %collective-permute-start.8 = (f32[16,3,1,128]{3,0,2,1:T(8,128)S(1)}, f32[16,3,1,128]{3,0,2,1:T(8,128)S(1)}, u32[]{:S(2)}, u32[]{:S(2)}) collective-permute-start(f32[16,3,1,128]{3,0,2,1:T(8,128)S(1)} %get-tuple-element.6), channel_id=1, source_target_pairs={{1,0},{2,1},{3,2},{4,3},{5,4},{6,5},{7,6},{8,7},{9,8},{10,9},{11,1... | collective-permute-start | bytes 73736 | tf_op jit(solution)/shard_map/ppermute | solution.py:19
  28.6 6.1 %collective-permute-start.9 = (f32[16,3,1,128]{3,0,2,1:T(8,128)S(1)}, f32[16,3,1,128]{3,0,2,1:T(8,128)S(1)}, u32[]{:S(2)}, u32[]{:S(2)}) collective-permute-start(f32[16,3,1,128]{3,0,2,1:T(8,128)S(1)} %get-tuple-element.7), channel_id=1, source_target_pairs={{0,1},{1,2},{2,3},{3,4},{4,5},{5,6},{6,7},{7,8},{8,9},{9,10},{10,1... | collective-permute-start | bytes 73736 | tf_op jit(solution)/shard_map/ppermute | solution.py:17
  35.0 1.6 %collective-permute-start.10 = (f32[16,3,1,128]{3,0,2,1:T(8,128)S(1)}, f32[16,3,1,128]{3,0,2,1:T(8,128)S(1)}, u32[]{:S(2)}, u32[]{:S(2)}) collective-permute-start(f32[16,3,1,128]{3,0,2,1:T(8,128)S(1)} %get-tuple-element.4), channel_id=1, source_target_pairs={{1,0},{2,1},{3,2},{4,3},{5,4},{6,5},{7,6},{8,7},{9,8},{10,9},{11,1... | collective-permute-start | bytes 73736 | tf_op jit(solution)/shard_map/ppermute | solution.py:19
  35.1 6.1 %collective-permute-start.11 = (f32[16,3,1,128]{3,0,2,1:T(8,128)S(1)}, f32[16,3,1,128]{3,0,2,1:T(8,128)S(1)}, u32[]{:S(2)}, u32[]{:S(2)}) collective-permute-start(f32[16,3,1,128]{3,0,2,1:T(8,128)S(1)} %get-tuple-element.5), channel_id=1, source_target_pairs={{0,1},{1,2},{2,3},{3,4},{4,5},{5,6},{6,7},{7,8},{8,9},{9,10},{10,1... | collective-permute-start | bytes 73736 | tf_op jit(solution)/shard_map/ppermute | solution.py:17
  41.4 1.6 %collective-permute-start.12 = (f32[16,3,1,128]{3,0,2,1:T(8,128)S(1)}, f32[16,3,1,128]{3,0,2,1:T(8,128)S(1)}, u32[]{:S(2)}, u32[]{:S(2)}) collective-permute-start(f32[16,3,1,128]{3,0,2,1:T(8,128)S(1)} %get-tuple-element.2), channel_id=1, source_target_pairs={{1,0},{2,1},{3,2},{4,3},{5,4},{6,5},{7,6},{8,7},{9,8},{10,9},{11,1... | collective-permute-start | bytes 73736 | tf_op jit(solution)/shard_map/ppermute | solution.py:19
  41.5 6.0 %collective-permute-start.13 = (f32[16,3,1,128]{3,0,2,1:T(8,128)S(1)}, f32[16,3,1,128]{3,0,2,1:T(8,128)S(1)}, u32[]{:S(2)}, u32[]{:S(2)}) collective-permute-start(f32[16,3,1,128]{3,0,2,1:T(8,128)S(1)} %get-tuple-element.3), channel_id=1, source_target_pairs={{0,1},{1,2},{2,3},{3,4},{4,5},{5,6},{6,7},{7,8},{8,9},{9,10},{10,1... | collective-permute-start | bytes 73736 | tf_op jit(solution)/shard_map/ppermute | solution.py:17
  51.2 12.5 %all-to-all-start = ((bf16[16,2,3072]{2,1,0:T(2,128)(2,1)}), bf16[16,2,3072]{2,1,0:T(2,128)(2,1)S(1)}, u32[]{:S(2)}, u32[]{:S(2)}) async-start(bf16[16,2,3072]{2,1,0:T(2,128)(2,1)} %reshape.53), calls=%async_computation | async-start | bytes 393216 | tf_op jit(solution)/shard_map/all_to_all | solution.py:82
  67.1 2.7 %copy-start = (bf16[64,3,8,256]{3,2,1,0:T(8,128)(2,1)S(1)}, bf16[64,3,8,256]{3,2,1,0:T(8,128)(2,1)}, u32[]{:S(2)}) copy-start(bf16[64,3,8,256]{3,2,1,0:T(8,128)(2,1)} %param.7) | copy-start | bytes 2359300
  67.1 34.0 %copy-start.3 = (f32[64]{0:T(128)S(1)}, f32[64]{0:T(128)}, u32[]{:S(2)}) copy-start(f32[64]{0:T(128)} %param.8) | copy-start | bytes 772
  101.1 0.6 copy-start.2
